TPU v7x, 32 devices: a whole 2x2x4 slice. The times are simulated.
32 devices in a mesh: cases: 2 (over y), nodes: 4 (over z), fsdp: 2 (over x), rep: 2 (over core).
Axes of the slice: x: 2, y: 2, z: 4, core: 2. Of those that a mesh axis runs over, the one named last changes fastest.
Arguments:
- features: bfloat16 [8, 1024, 512], P(('cases', 'fsdp', 'rep'), 'nodes'), parts along dimension 0
- cotangent: bfloat16 [8, 1024, 512], P(('cases', 'fsdp', 'rep'), 'nodes'), parts along dimension 0
- weights: bfloat16 [2, 2, 512, 512], P(None, None, 'fsdp'), may hold values from -0.25 to 0.25
- gains: float32 [2, 512], replicated, may hold values from 0.25 to 1.75
- tile_pairs: int32 [4, 2, 12], P('nodes'), may hold values from 0 to 3, as said below
- halo_send: int32 [4, 2, 1], P('nodes'), may hold values from 0 to 1, as said below
- entry_counts: int32 [4], P('nodes'), may hold values from 2 to 12, as said below
- tile_values: bfloat16 [4, 12, 128, 128], P('nodes'), may hold values from -0.375 to 0.375
Outputs:
- output: bfloat16 [8, 1024, 512], P(('cases', 'fsdp', 'rep'), 'nodes'), parts along dimension 0
- weight_grads: float32 [512, 4, 2, 512], P('fsdp', 'cases'), parts along dimension 1
- gain_grads: float32 [4, 512], P('cases'), parts along dimension 0
There are 2 independent parts, one for each index of `cases`. A program takes and returns all parts, laid end to end along the dimension named above; an argument that names none is the same for every part. Nothing has to cross between parts.
Inputs may be any that keep to these rules, and one draw needn't show every extreme that they name: `tile_pairs`: entries 0 to 1 of every partition name the column tiles 2 to 3 in order; row tiles are below 2. Each list halo_send[q, k] holds 1 distinct tiles. `entry_counts`: exactly one partition has all 12 entries live; every other one at most 6.
All inputs are finite; a program needn't handle non-finite values.
Results may differ from a plain program's by a relative error of at most 0.014.
Values may be sent and summed in bfloat16 or wider, within the bound.
A program may use at most 64 MiB of HBM per device.

v0:
```python
import jax
import jax.numpy as jnp
from jax import lax
from jax.sharding import PartitionSpec as P

EPSILON = 1e-05


def with_halo(x, sides, width):
    for axis, dim in sides:
        count, length = (lax.axis_size(axis), x.shape[dim])
        up = [(i, (i + 1) % count) for i in range(count - 1)]
        down = [(j, i) for i, j in up]
        last = lax.slice_in_dim(x, length - width, length, axis=dim)
        first = lax.slice_in_dim(x, 0, width, axis=dim)
        before = lax.ppermute(last, axis, up)
        after = lax.ppermute(first, axis, down)
        x = jnp.concatenate([before, x, after], axis=dim)
    return x


def silu_slope(values):
    sigmoid_part = jax.nn.sigmoid(values)
    return sigmoid_part * (1.0 + values * (1.0 - sigmoid_part))


def tile_sweep(count, values, target_ids, source_ids, sources, shape, transposed):

    def step(entry, summed):
        tile_matrix = lax.dynamic_index_in_dim(values, entry, 0, keepdims=False)
        source_id = lax.dynamic_index_in_dim(source_ids, entry, 0, keepdims=False)
        target_id = lax.dynamic_index_in_dim(target_ids, entry, 0, keepdims=False)
        source_tile = lax.dynamic_index_in_dim(sources, source_id, 1, keepdims=False)
        if transposed:
            term = jnp.einsum(
                "ij,sid->sjd", tile_matrix, source_tile, preferred_element_type=jnp.float32
            )
        else:
            term = jnp.einsum(
                "ij,sjd->sid", tile_matrix, source_tile, preferred_element_type=jnp.float32
            )
        present = lax.dynamic_index_in_dim(summed, target_id, 1, keepdims=True)
        return lax.dynamic_update_index_in_dim(summed, present + term[:, None], target_id, 1)

    return lax.fori_loop(0, count, step, jnp.zeros(shape, jnp.float32))


def body(features, cotangent, weights, gains, tile_pairs, halo_send, entry_counts, tile_values):
    samples_dev, rows_dev, width = features.shape
    layer_count = weights.shape[0]
    tile_size = tile_values.shape[-1]
    local_tiles = rows_dev // tile_size
    sends = halo_send[0]
    halo_count = sends.shape[1]
    rim_rows = halo_count * tile_size
    row_ids = tile_pairs[0, 0]
    col_ids = tile_pairs[0, 1]
    count = entry_counts[0]
    values = tile_values[0]
    flat_rows = samples_dev * rows_dev
    send_order = jnp.concatenate([sends[0], sends[1]])
    picks = (send_order[:, None] == jnp.arange(local_tiles, dtype=jnp.int32)[None, :]).astype(
        jnp.float32
    )
    current = features
    saved = []
    for layer_id in range(layer_count):
        widened = current.astype(jnp.float32)
        inv_rms = lax.rsqrt(jnp.mean(widened * widened, axis=-1, keepdims=True) + EPSILON)
        normed = (widened * inv_rms * gains[layer_id]).astype(jnp.bfloat16)
        flat_normed = normed.reshape(flat_rows, width)
        pair = weights[layer_id]
        products = jnp.einsum(
            "nk,wkd->wnd",
            flat_normed,
            lax.all_gather(pair, "fsdp", axis=1, tiled=True),
            preferred_element_type=jnp.float32,
        )
        messages = (
            products[1].astype(jnp.bfloat16).reshape(samples_dev, local_tiles, tile_size, width)
        )
        outgoing = jnp.concatenate(
            [jnp.take(messages, sends[0], axis=1), jnp.take(messages, sends[1], axis=1)], axis=1
        )
        outgoing = outgoing.reshape(samples_dev, 2 * rim_rows, width)
        extended = with_halo(outgoing, (("nodes", 1),), rim_rows)
        lower_rim = extended[:, :rim_rows].reshape(samples_dev, halo_count, tile_size, width)
        upper_rim = extended[:, rim_rows * 3 :].reshape(samples_dev, halo_count, tile_size, width)
        columns_all = jnp.concatenate([messages, lower_rim, upper_rim], axis=1)
        summed = tile_sweep(
            count,
            values,
            row_ids,
            col_ids,
            columns_all,
            (samples_dev, local_tiles, tile_size, width),
            False,
        )
        before = products[0].reshape(samples_dev, rows_dev, width) + summed.reshape(
            samples_dev, rows_dev, width
        )
        saved.append((widened, inv_rms, flat_normed, before))
        current = (widened + jax.nn.silu(before)).astype(jnp.bfloat16)
    upstream = cotangent.astype(jnp.float32)
    grad_pieces = [None] * layer_count
    gain_pieces = [None] * layer_count
    for layer_id in reversed(range(layer_count)):
        widened, inv_rms, flat_normed, before = saved[layer_id]
        slope = (upstream * silu_slope(before)).astype(jnp.bfloat16)
        slope_tiles = slope.reshape(samples_dev, local_tiles, tile_size, width)
        returned = tile_sweep(
            count,
            values,
            col_ids,
            row_ids,
            slope_tiles,
            (samples_dev, local_tiles + 2 * halo_count, tile_size, width),
            True,
        )
        border = returned[:, local_tiles:].reshape(samples_dev, 2 * rim_rows, width)
        arrived = with_halo(border.astype(jnp.bfloat16), (("nodes", 1),), rim_rows).astype(
            border.dtype
        )
        incoming = jnp.concatenate([arrived[:, :rim_rows], arrived[:, rim_rows * 3 :]], axis=1)
        incoming = incoming.reshape(samples_dev, 2 * halo_count, tile_size, width)
        own_tiles = returned[:, :local_tiles] + jnp.einsum(
            "kt,sknd->stnd", picks, incoming, precision=lax.Precision.HIGHEST
        )
        back_messages = own_tiles.astype(jnp.bfloat16).reshape(flat_rows, width)
        flat_slope = slope.reshape(flat_rows, width)
        pair = weights[layer_id]
        project_piece = lax.all_gather(pair, "fsdp", axis=1, tiled=True)
        dnormed = jnp.einsum(
            "nd,kd->nk", flat_slope, project_piece[0], preferred_element_type=jnp.float32
        ) + jnp.einsum(
            "nd,kd->nk", back_messages, project_piece[1], preferred_element_type=jnp.float32
        )
        dnormed = dnormed.reshape(samples_dev, rows_dev, width)
        gain_pieces[layer_id] = jnp.sum(dnormed * widened * inv_rms, axis=(0, 1))
        grad_pieces[layer_id] = (flat_normed, flat_slope, back_messages)
        if layer_id > 0:
            scaled = dnormed * gains[layer_id]
            mean_part = jnp.mean(scaled * widened, axis=-1, keepdims=True)
            upstream = (
                upstream + inv_rms * scaled - widened * (inv_rms * inv_rms * inv_rms) * mean_part
            )
    select_columns = lambda matrix: matrix
    blocks = []
    for layer_id in range(layer_count):
        normed_rows, slope_rows, message_rows = grad_pieces[layer_id]
        chosen = select_columns(normed_rows)
        blocks.append(
            jnp.einsum("nk,nd->kd", chosen, slope_rows, preferred_element_type=jnp.float32)
        )
        blocks.append(
            jnp.einsum("nk,nd->kd", chosen, message_rows, preferred_element_type=jnp.float32)
        )
    reduced_rows = lax.psum_scatter(
        jnp.concatenate(blocks, axis=1).astype(jnp.bfloat16),
        "fsdp",
        scatter_dimension=0,
        tiled=True,
    ).astype(jnp.float32)
    weight_sum = lax.psum(reduced_rows, ("nodes", "rep"))
    weight_grads = weight_sum.reshape(weight_sum.shape[0], layer_count, 2, width)
    gain_grads = lax.psum(jnp.stack(gain_pieces), ("nodes", "fsdp", "rep"))
    return (current, weight_grads, gain_grads)


def solution(mesh):
    placed = (
        P(("cases", "fsdp", "rep"), "nodes", None),
        P(("cases", "fsdp", "rep"), "nodes", None),
        P(None, None, "fsdp", None),
        P(),
        P("nodes", None, None),
        P("nodes", None, None),
        P("nodes"),
        P("nodes", None, None, None),
    )
    return jax.shard_map(
        body,
        mesh=mesh,
        in_specs=placed,
        out_specs=(
            P(("cases", "fsdp", "rep"), "nodes", None),
            P("fsdp", "cases", None, None),
            P("cases", None),
        ),
        check_vma=False,
    )
```

profile of v0, /device:TPU:0, one launch (start us, length us, event | category | flops | bytes accessed | tf_op | source)
XLA Modules:
  0.0 533.9 jit_solution(6361137757923750617)
XLA Ops:
  7.2 2.3 fusion.77
  9.6 0.7 all-gather.7.cloned.1.call-update
  10.3 0.7 fusion.83
  15.0 19.1 %all-gather.5.cloned.1.call-done = bf16[1,2,512,512]{3,2,1,0:T(8,128)(2,1)} async-done(((bf16[1,2,256,512]{3,2,1,0:T(8,128)(2,1)}), bf16[1,2,512,512]{3,2,1,0:T(8,128)(2,1)}) %all-gather.5.cloned.1.call-update) | async-done | bytes 1048592 | tf_op jit(solution)/shard_map/all_gather | solution.py:76
  34.2 1.7 convolution_bitcast_fusion.5
  36.1 3.4 collective-permute-start
  39.5 1.3 collective-permute-start.1
  40.8 1.4 collective-permute-done
  42.2 4.1 collective-permute-done.1
  46.5 14.4 %while.41 = (s32[]{:T(128)}, f32[1,2,128,512]{3,2,1,0:T(8,128)S(1)}, s32[]{:T(128)}, s32[12]{0:T(128)S(1)}, s32[12]{0:T(128)S(1)}, /*index=5*/bf16[1,4,128,512]{...) while((s32[]{:T(128)}, ...), condition=%wide.region_2.4_spmd, body=%wide.region_1.0_spmd.sunk | while | flops 16842764 | bytes 2785539 | solution.py:45
  47.1 0.6 dynamic_slice.125
  49.7 0.6 dynamic_slice.126
  52.2 1.0 fusion.102
  54.0 0.6 dynamic_slice.125
  56.6 0.6 dynamic_slice.126
  59.1 1.0 fusion.102
  61.2 1.7 convolution_bitcast_fusion.4
  63.1 10.3 %collective-permute-start.2 = (bf16[1,128,512]{2,1,0:T(8,128)(2,1)S(1)}, bf16[1,128,512]{2,1,0:T(8,128)(2,1)S(1)}, u32[]{:S(2)}, u32[]{:S(2)}) collective-permute-start(bf16[1,128,512]{2,1,0:T(8,128)(2,1)S(1)} %get-tuple-element.243), channel_id=1, source_target_pairs={{0,4},{4,8},{8,12},{1,5},{5,9},{9,13},{2,6},{6,10},{10,14},{3,7},{... | collective-permute-start | bytes 393224 | tf_op jit(solution)/shard_map/ppermute | solution.py:16
  73.4 1.3 collective-permute-start.3
  74.7 1.4 pad_add_fusion
  76.0 4.2 collective-permute-done.3
  80.2 0.9 pad_maximum_fusion.2
  81.2 15.1 %while.42 = (s32[]{:T(128)}, f32[1,2,128,512]{3,2,1,0:T(8,128)S(1)}, s32[]{:T(128)}, s32[12]{0:T(128)S(1)}, s32[12]{0:T(128)S(1)}, /*index=5*/bf16[1,4,128,512]{...) while((s32[]{:T(128)}, ...), condition=%wide.region_5.7_spmd, body=%wide.region_4.6_spmd.sunk | while | flops 16842764 | bytes 2785539 | solution.py:45
  81.9 0.6 dynamic_slice.130
  84.6 0.6 dynamic_slice.131
  87.1 1.1 fusion.105
  89.1 0.6 dynamic_slice.130
  91.8 0.6 dynamic_slice.131
  94.3 1.1 fusion.105
  96.3 1.0 fusion.30
  97.4 14.7 %while.43 = (s32[]{:T(128)}, f32[1,4,128,512]{3,2,1,0:T(8,128)S(1)}, s32[]{:T(128)}, s32[12]{0:T(128)S(1)}, s32[12]{0:T(128)S(1)}, /*index=5*/bf16[1,2,128,512]{...) while((s32[]{:T(128)}, ...), condition=%wide.region_7.9_spmd, body=%wide.region_6.8_spmd.sunk | while | flops 16842764 | bytes 2785539 | solution.py:45
  98.0 0.6 dynamic_slice.135
  100.7 0.6 dynamic_slice.136
  103.3 1.0 fusion.108
  105.1 0.6 dynamic_slice.135
  107.8 0.6 dynamic_slice.136
  110.3 1.0 fusion.108
  112.2 77.1 %collective-permute-start.4 = (bf16[1,128,512]{2,1,0:T(8,128)(2,1)S(1)}, bf16[1,128,512]{2,1,0:T(8,128)(2,1)S(1)}, u32[]{:S(2)}, u32[]{:S(2)}) collective-permute-start(bf16[1,128,512]{2,1,0:T(8,128)(2,1)S(1)} %get-tuple-element.241), channel_id=1, source_target_pairs={{0,4},{4,8},{8,12},{1,5},{5,9},{9,13},{2,6},{6,10},{10,14},{3,7},{... | collective-permute-start | bytes 393224 | tf_op jit(solution)/shard_map/ppermute | solution.py:16
  189.3 1.3 collective-permute-start.5
  190.6 1.4 fusion.47
  192.0 0.4 convolution_convert_fusion.1
  192.4 3.8 collective-permute-done.5
  196.3 1.3 fusion.52
  197.7 0.5 fusion.45
  198.6 1.2 convolution_convert_fusion.3
  199.9 14.7 %while.44 = (s32[]{:T(128)}, f32[1,4,128,512]{3,2,1,0:T(8,128)S(1)}, s32[]{:T(128)}, s32[12]{0:T(128)S(1)}, s32[12]{0:T(128)S(1)}, /*index=5*/bf16[1,2,128,512]{...) while((s32[]{:T(128)}, ...), condition=%wide.region_10.12_spmd, body=%wide.region_9.11_spmd.sunk | while | flops 16842764 | bytes 2785539 | solution.py:45
  200.6 0.6 dynamic_slice.140
  203.3 0.6 dynamic_slice.141
  205.8 1.0 fusion.111
  207.6 0.6 dynamic_slice.140
  210.3 0.6 dynamic_slice.141
  212.8 1.0 fusion.111
  214.7 136.6 %collective-permute-start.6 = (bf16[1,128,512]{2,1,0:T(8,128)(2,1)S(1)}, bf16[1,128,512]{2,1,0:T(8,128)(2,1)S(1)}, u32[]{:S(2)}, u32[]{:S(2)}) collective-permute-start(bf16[1,128,512]{2,1,0:T(8,128)(2,1)S(1)} %get-tuple-element.239), channel_id=1, source_target_pairs={{0,4},{4,8},{8,12},{1,5},{5,9},{9,13},{2,6},{6,10},{10,14},{3,7},{... | collective-permute-start | bytes 393224 | tf_op jit(solution)/shard_map/ppermute | solution.py:16
  351.4 1.3 collective-permute-start.7
  353.1 0.8 collective-permute-done.6
  353.9 4.4 collective-permute-done.7
  358.3 1.3 fusion.50
  359.8 0.4 convolution_convert_fusion.2
  360.2 1.5 pad_maximum_fusion
  361.7 93.0 %reduce-scatter.2.cloned.1.call-done = bf16[256,2048]{0,1:T(8,128)(2,1)} async-done(((bf16[512,2048]{0,1:T(8,128)(2,1)}), bf16[256,2048]{0,1:T(8,128)(2,1)}) %reduce-scatter.2.cloned.1.call-update) | async-done | bytes 1048592 | tf_op jit(solution)/shard_map/reduce_scatter | solution.py:158
  454.8 3.9 copy.37
  459.4 33.5 %psum.15 = f32[2,512]{1,0:T(2,128)} all-reduce(f32[2,512]{1,0:T(2,128)S(1)} %pad_maximum_fusion.11), channel_id=1, replica_groups=mesh['cases'=2,'nodes'=4,'fsdp'=2,'rep'=2] {'nodes','fsdp','rep'}, use_global_device_ids=true, to_apply=%region_15.17 | all-reduce | flops 1024 | bytes 8192 | tf_op jit(solution)/shard_map/psum | solution.py:166
  492.9 30.9 %all-reduce.2.cloned.1.call-done = f32[256,2,2,512]{3,2,1,0:T(2,128)} async-done(((f32[256,2,2,512]{3,2,1,0:T(2,128)}), f32[256,2,2,512]{3,2,1,0:T(2,128)}) %all-reduce.2.cloned.1.call-update) | async-done | bytes 2097168 | tf_op jit(solution)/shard_map/psum | solution.py:164
  523.8 3.6 copy.106
  (97 shorter events, 5.7 us)
Async XLA Ops:
  7.2 3.2 copy-start.8
  7.2 7.7 %copy-start.7 = (f32[2,512]{1,0:T(2,128)S(1)}, f32[2,512]{1,0:T(2,128)}, u32[]{:S(2)}) copy-start(f32[2,512]{1,0:T(2,128)} %param.21) | copy-start | bytes 12292
  7.2 7.7 %copy-start = (bf16[1,256,512]{2,1,0:T(8,128)(2,1)S(1)}, bf16[1,256,512]{2,1,0:T(8,128)(2,1)}, u32[]{:S(2)}) copy-start(bf16[1,256,512]{2,1,0:T(8,128)(2,1)} %param.18) | copy-start | bytes 786436
  7.2 27.0 %all-gather.5.cloned.1.call-start = ((), (), s32[]{:S(2)}) async-start(), calls=%async_computation.3 | async-start | bytes 1572864 | tf_op jit(solution)/shard_map/all_gather | solution.py:76
  9.5 51.7 %all-gather.7.cloned.1.call-start = ((), (), s32[]{:S(2)}) async-start(), calls=%async_computation.4 | async-start | bytes 1572864 | tf_op jit(solution)/shard_map/all_gather | solution.py:76
  10.3 444.5 %reduce-scatter.2.cloned.1.call-start = ((), (), s32[]{:S(2)}) async-start(), calls=%async_computation.1 | async-start | bytes 3145728 | tf_op jit(solution)/shard_map/reduce_scatter | solution.py:158
  34.2 6.6 %copy-start.9 = (s32[1,2,12]{2,1,0:T(2,128)S(1)}, s32[1,2,12]{2,1,0:T(2,128)}, u32[]{:S(2)}) copy-start(s32[1,2,12]{2,1,0:T(2,128)} %param.22) | copy-start | bytes 292
  35.9 25.0 %copy-start.1 = (f32[2,256,512]{2,1,0:T(8,128)}, f32[2,256,512]{2,1,0:T(8,128)S(1)}, u32[]{:S(2)}) copy-start(f32[2,256,512]{2,1,0:T(8,128)S(1)} %convolution_bitcast_fusion.5) | copy-start | bytes 3145732
  36.1 6.1 %collective-permute-start = (bf16[1,128,512]{2,1,0:T(8,128)(2,1)S(1)}, bf16[1,128,512]{2,1,0:T(8,128)(2,1)S(1)}, u32[]{:S(2)}, u32[]{:S(2)}) collective-permute-start(bf16[1,128,512]{2,1,0:T(8,128)(2,1)S(1)} %get-tuple-element.247), channel_id=1, source_target_pairs={{0,4},{4,8},{8,12},{1,5},{5,9},{9,13},{2,6},{6,10},{10,14},{3,7},{... | collective-permute-start | bytes 393224 | tf_op jit(solution)/shard_map/ppermute | solution.py:16
  39.5 6.9 %collective-permute-start.1 = (bf16[1,128,512]{2,1,0:T(8,128)(2,1)S(1)}, bf16[1,128,512]{2,1,0:T(8,128)(2,1)S(1)}, u32[]{:S(2)}, u32[]{:S(2)}) collective-permute-start(bf16[1,128,512]{2,1,0:T(8,128)(2,1)S(1)} %get-tuple-element.248), channel_id=1, source_target_pairs={{4,0},{8,4},{12,8},{5,1},{9,5},{13,9},{6,2},{10,6},{14,10},{7,3},{... | collective-permute-start | bytes 393224 | tf_op jit(solution)/shard_map/ppermute | solution.py:17
  63.1 12.9 %collective-permute-start.2 = (bf16[1,128,512]{2,1,0:T(8,128)(2,1)S(1)}, bf16[1,128,512]{2,1,0:T(8,128)(2,1)S(1)}, u32[]{:S(2)}, u32[]{:S(2)}) collective-permute-start(bf16[1,128,512]{2,1,0:T(8,128)(2,1)S(1)} %get-tuple-element.243), channel_id=1, source_target_pairs={{0,4},{4,8},{8,12},{1,5},{5,9},{9,13},{2,6},{6,10},{10,14},{3,7},{... | collective-permute-start | bytes 393224 | tf_op jit(solution)/shard_map/ppermute | solution.py:16
  73.4 6.9 %collective-permute-start.3 = (bf16[1,128,512]{2,1,0:T(8,128)(2,1)S(1)}, bf16[1,128,512]{2,1,0:T(8,128)(2,1)S(1)}, u32[]{:S(2)}, u32[]{:S(2)}) collective-permute-start(bf16[1,128,512]{2,1,0:T(8,128)(2,1)S(1)} %get-tuple-element.244), channel_id=1, source_target_pairs={{4,0},{8,4},{12,8},{5,1},{9,5},{13,9},{6,2},{10,6},{14,10},{7,3},{... | collective-permute-start | bytes 393224 | tf_op jit(solution)/shard_map/ppermute | solution.py:17
  81.2 15.1 %copy-start.6 = (bf16[1,256,512]{2,1,0:T(8,128)(2,1)S(1)}, bf16[1,256,512]{2,1,0:T(8,128)(2,1)}, u32[]{:S(2)}) copy-start(bf16[1,256,512]{2,1,0:T(8,128)(2,1)} %param.19) | copy-start | bytes 786436
  112.2 80.2 %collective-permute-start.4 = (bf16[1,128,512]{2,1,0:T(8,128)(2,1)S(1)}, bf16[1,128,512]{2,1,0:T(8,128)(2,1)S(1)}, u32[]{:S(2)}, u32[]{:S(2)}) collective-permute-start(bf16[1,128,512]{2,1,0:T(8,128)(2,1)S(1)} %get-tuple-element.241), channel_id=1, source_target_pairs={{0,4},{4,8},{8,12},{1,5},{5,9},{9,13},{2,6},{6,10},{10,14},{3,7},{... | collective-permute-start | bytes 393224 | tf_op jit(solution)/shard_map/ppermute | solution.py:16
  189.3 6.9 %collective-permute-start.5 = (bf16[1,128,512]{2,1,0:T(8,128)(2,1)S(1)}, bf16[1,128,512]{2,1,0:T(8,128)(2,1)S(1)}, u32[]{:S(2)}, u32[]{:S(2)}) collective-permute-start(bf16[1,128,512]{2,1,0:T(8,128)(2,1)S(1)} %get-tuple-element.242), channel_id=1, source_target_pairs={{4,0},{8,4},{12,8},{5,1},{9,5},{13,9},{6,2},{10,6},{14,10},{7,3},{... | collective-permute-start | bytes 393224 | tf_op jit(solution)/shard_map/ppermute | solution.py:17
  192.4 5.3 copy-start.3
  196.3 2.0 copy-start.2
  214.7 139.1 %collective-permute-start.6 = (bf16[1,128,512]{2,1,0:T(8,128)(2,1)S(1)}, bf16[1,128,512]{2,1,0:T(8,128)(2,1)S(1)}, u32[]{:S(2)}, u32[]{:S(2)}) collective-permute-start(bf16[1,128,512]{2,1,0:T(8,128)(2,1)S(1)} %get-tuple-element.239), channel_id=1, source_target_pairs={{0,4},{4,8},{8,12},{1,5},{5,9},{9,13},{2,6},{6,10},{10,14},{3,7},{... | collective-permute-start | bytes 393224 | tf_op jit(solution)/shard_map/ppermute | solution.py:16
  351.4 6.9 %collective-permute-start.7 = (bf16[1,128,512]{2,1,0:T(8,128)(2,1)S(1)}, bf16[1,128,512]{2,1,0:T(8,128)(2,1)S(1)}, u32[]{:S(2)}, u32[]{:S(2)}) collective-permute-start(bf16[1,128,512]{2,1,0:T(8,128)(2,1)S(1)} %get-tuple-element.240), channel_id=1, source_target_pairs={{4,0},{8,4},{12,8},{5,1},{9,5},{13,9},{6,2},{10,6},{14,10},{7,3},{... | collective-permute-start | bytes 393224 | tf_op jit(solution)/shard_map/ppermute | solution.py:17
  358.3 1.9 copy-start.5
  361.7 162.1 %all-reduce.2.cloned.1.call-start = ((), (), s32[]{:S(2)}) async-start(), calls=%async_computation.2 | async-start | bytes 4194304 | tf_op jit(solution)/shard_map/psum | solution.py:164
  454.8 3.9 copy-start.4
Sparse Core Ops, SparseCore 0:
  10.1 23.9 all-gather.4
  35.7 21.2 all-gather.6
  361.8 92.9 reduce-scatter.1
  458.8 64.9 all-reduce.1
where the time goes:
time: 540 us; the launch traced here: 534 us
  starting transfers between devices  233 us (43%)
  waiting for transfers between devices  162 us (30%)
  loops' own time  39.1 us (7%)
  blocking collectives  33.5 us (6%)
  local copies, waits for them, and re-layouts  22.8 us (4%)
  matrix products  19 us (4%)
  between operations  18.2 us (3%)
  other arithmetic  6.09 us (1%)
    ppermute x4, starting transfers between devices, with_halo(): before = lax.ppermute(last, axis, up)  227 us
    reduce_scatter x1, waiting for transfers between devices, body(): lax.psum_scatter(jnp.concatenate(blocks, axis=1).astype(jnp.bfloat16), 'f...  93 us
    another operation x4, loops' own time, tile_sweep(): return lax.fori_loop(0, count, step, jnp.zeros(shape, jnp.float32))  39.1 us
    psum x1, blocking collectives, body(): gain_grads = lax.psum(jnp.stack(gain_pieces), ('nodes', 'fsdp', 'rep'))  33.5 us
    psum x1, waiting for transfers between devices, body(): weight_sum = lax.psum(reduced_rows, ('nodes', 'rep'))  30.9 us
    all_gather x2, waiting for transfers between devices, body(): lax.all_gather(pair, 'fsdp', axis=1, tiled=True)  19.2 us
    ppermute x4, waiting for transfers between devices, with_halo(): after = lax.ppermute(first, axis, down)  16.5 us
  transfers between devices with their start and end apart: 12, of which 9 were waited for; matrix products, arithmetic and copies ran while one was open for 2% of the time, Pallas kernels for 0%

commit v1 on v0

v1 whole, which is shorter than its diff:
```python
import functools

import jax
import jax.numpy as jnp
from jax import lax
from jax.experimental import pallas as pl
from jax.experimental.pallas import tpu as pltpu
from jax.sharding import PartitionSpec as P

MESH = pl.DeviceIdType.MESH
EPSILON = 1e-05
F32 = jnp.float32
BF16 = jnp.bfloat16


def mm(a, b):
    return lax.dot_general(a, b, (((1,), (0,)), ((), ())), preferred_element_type=F32)


def mm_bt(a, b):
    return lax.dot_general(a, b, (((1,), (1,)), ((), ())), preferred_element_type=F32)


def mm_at(a, b):
    return lax.dot_general(a, b, (((0,), (0,)), ((), ())), preferred_element_type=F32)


def kernel(
    nz, nx, chunk, owners,
    x_ref, cot_ref, w_ref, gains_ref, pairs_ref, hs_ref, cnt_ref, tv_ref,
    out_ref, wg_ref, gg_ref,
    wfull, xs, inv_s, normed_s, before_s, adj, adj_t, msgs,
    xsend, xrecv, rsend, rrecv, slope_s, back_s, own_s,
    ga_send, ga_recv, ga_own, gb_send, gb_recv, gb_own, gc_send, gc_recv, gd,
    hg_own, hg_a, hg_b, hg_c,
    w_ss, w_rs, f_ss, f_rs, x_ss, x_rs, r_ss, r_rs,
    a_ss, a_rs, b_ss, b_rs, c_ss, c_rs, d_ss, d_rs, e_ss, e_rs, h_ss, h_rs,
):
    layers, _, width, _ = wfull.shape
    tile = tv_ref.shape[-1]
    tiles = xs.shape[1]
    rows = tiles * tile
    cols = tiles + 2
    half = width // 2
    depth = width // nx
    z = lax.axis_index("nodes")
    xi = lax.axis_index("fsdp")
    r = lax.axis_index("rep")
    sib = {"rep": 1 - r}

    def remote(src, dst, ss, rs, dev):
        return pltpu.make_async_remote_copy(
            src_ref=src, dst_ref=dst, send_sem=ss, recv_sem=rs, device_id=dev, device_id_type=MESH
        )

    def xpeer(d):
        return lax.rem(xi + d, nx)

    def xfrom(d):
        return lax.rem(xi + nx - d, nx)

    def zpeer(d):
        return lax.rem(z + d, nz)

    def zfrom(d):
        return lax.rem(z + nz - d, nz)

    barrier = pltpu.get_barrier_semaphore()
    pl.semaphore_signal(barrier, inc=1, device_id=sib, device_id_type=MESH)
    for d in range(1, nx):
        pl.semaphore_signal(barrier, inc=1, device_id={"fsdp": xpeer(d)}, device_id_type=MESH)
    for d in range(1, nz):
        pl.semaphore_signal(barrier, inc=1, device_id={"nodes": zpeer(d)}, device_id_type=MESH)

    has_low = z > 0
    has_high = z < nz - 1

    def halo(send, recv, ss, rs, l):
        low = remote(send.at[l, 0], recv.at[l, 1], ss.at[l, 0], rs.at[l, 1], {"nodes": jnp.maximum(z - 1, 0)})
        high = remote(send.at[l, 1], recv.at[l, 0], ss.at[l, 1], rs.at[l, 0], {"nodes": jnp.minimum(z + 1, nz - 1)})
        return low, high

    def halo_start(copies):
        pl.when(has_low)(copies[0].start)
        pl.when(has_high)(copies[1].start)

    def halo_wait(copies):
        def low():
            copies[0].wait_send()
            copies[1].wait_recv()

        def high():
            copies[1].wait_send()
            copies[0].wait_recv()

        pl.when(has_low)(low)
        pl.when(has_high)(high)

    xs[0] = x_ref[0].reshape(tiles, tile, width)
    for k, outermost in ((0, z == 0), (1, z == nz - 1)):

        @pl.when(outermost)
        def clear(k=k):
            for l in range(layers):
                xrecv[l, k] = jnp.zeros((tile, width), BF16)
                rrecv[l, k] = jnp.zeros((tile, width), BF16)

    for k in range(2):
        xsend[0, k] = xs[0, hs_ref[0, k, 0]]

    for l in range(layers):
        for w in range(2):
            wfull[l, w, pl.ds(pl.multiple_of(xi * depth, depth), depth), :] = w_ref[l, w]
    pl.semaphore_wait(barrier, 1 + (nx - 1) + (nz - 1))
    xcopies = [halo(xsend, xrecv, x_ss, x_rs, l) for l in range(layers)]
    rcopies = [halo(rsend, rrecv, r_ss, r_rs, l) for l in range(layers)]
    halo_start(xcopies[0])

    def part(l, w, owner):
        return wfull.at[l, w, pl.ds(pl.multiple_of(owner * depth, depth), depth), :]

    gathers = []
    forwards = []
    for l in range(layers):
        for d in range(1, nx):
            g = remote(w_ref.at[l, r], part(l, r, xi), w_ss.at[l, d], w_rs.at[l, d], {"fsdp": xpeer(d)})
            g.start()
            gathers.append(g)
            forwards.append(remote(part(l, r, xfrom(d)), part(l, r, xfrom(d)), f_ss.at[l, d], f_rs.at[l, d], sib))

    count = cnt_ref[0]

    def build(step, carry):
        i = step // cols
        c = lax.rem(step, cols)
        there = jnp.logical_and(
            jnp.logical_or(c != tiles, has_low), jnp.logical_or(c != tiles + 1, has_high)
        )
        total = jnp.zeros((tile, tile), F32)
        for e in range(tv_ref.shape[1]):
            hit = (pairs_ref[0, 0, e] == i) & (pairs_ref[0, 1, e] == c) & (e < count) & there
            total += jnp.where(hit, 1.0, 0.0).astype(F32) * tv_ref[0, e].astype(F32)
        at_i = pl.ds(pl.multiple_of(i * tile, tile), tile)
        at_c = pl.ds(pl.multiple_of(c * tile, tile), tile)
        adj[at_i, at_c] = total.astype(BF16)
        adj_t[at_c, at_i] = total.T.astype(BF16)
        return carry

    lax.fori_loop(0, tiles * cols, build, 0)

    def norm(v, l):
        inv = lax.rsqrt(jnp.mean(v * v, axis=-1, keepdims=True) + EPSILON)
        return inv, (v * inv * gains_ref[l : l + 1, :]).astype(BF16)

    for l in range(layers):
        wide = xs[l].reshape(rows, width).astype(F32)
        inv, normed = norm(wide, l)
        inv_s[l] = inv
        normed_s[l] = normed
        for d in range(nx - 1):
            gathers[l * (nx - 1) + d].wait_recv()
            forwards[l * (nx - 1) + d].start()
        own_first = mm(normed, wfull[l, 0]) if nx == 1 else None
        for d in range(1, nx):
            remote(
                part(l, 1 - r, xfrom(d)), part(l, 1 - r, xfrom(d)), f_ss.at[l, d], f_rs.at[l, d], sib
            ).wait_recv()
        direct = mm(normed, wfull[l, 0]) if own_first is None else own_first
        msgs[0:rows, :] = mm(normed, wfull[l, 1]).astype(BF16)
        halo_wait(xcopies[l])
        _, rim = norm(xrecv[l].reshape(2 * tile, width).astype(F32), l)
        msgs[rows:, :] = mm(rim, wfull[l, 1]).astype(BF16)
        before = direct + mm(adj[...], msgs[...])
        before_s[l] = before
        new = (wide + before / (1.0 + jnp.exp(-before))).astype(BF16)
        if l + 1 < layers:
            xs[l + 1] = new.reshape(tiles, tile, width)
            for k in range(2):
                xsend[l + 1, k] = xs[l + 1, hs_ref[0, k, 0]]
            halo_start(xcopies[l + 1])
        else:
            out_ref[0] = new

    mine = pl.ds(pl.multiple_of(r * half, half), half)
    other = pl.ds(pl.multiple_of((1 - r) * half, half), half)
    blocks = [(l, w) for l in reversed(range(layers)) for w in range(2)]

    a_copies, b_copies, c_copies, d_copies, e_copies = {}, {}, {}, {}, {}

    def stage_a(b):
        l, w = blocks[b]
        source = (slope_s, back_s)[w]
        left = normed_s[l]
        ga_send[b] = mm_at(left, source[l, :, other]).astype(BF16)
        a_copies[b] = remote(ga_send.at[b], ga_recv.at[b], a_ss.at[b], a_rs.at[b], sib)
        a_copies[b].start()
        ga_own[b] = mm_at(left, source[l, :, mine])

    def stage_b(b):
        a_copies[b].wait_recv()
        b_copies[b] = []
        for d in range(1, nx):
            at = pl.ds(pl.multiple_of(xpeer(d) * depth, depth), depth)
            gb_send[b, d] = (ga_own[b, at, :] + ga_recv[b, at, :].astype(F32)).astype(BF16)
            copy = remote(gb_send.at[b, d], gb_recv.at[b, d], b_ss.at[b, d], b_rs.at[b, d], {"fsdp": xpeer(d)})
            copy.start()
            b_copies[b].append(copy)
        at = pl.ds(pl.multiple_of(xi * depth, depth), depth)
        gb_own[b] = ga_own[b, at, :] + ga_recv[b, at, :].astype(F32)

    def span(owner):
        return pl.ds(pl.multiple_of(owner * chunk, chunk), chunk)

    def stage_c(b):
        total = gb_own[b]
        for d in range(1, nx):
            b_copies[b][d - 1].wait_recv()
            total = total + gb_recv[b, d].astype(F32)
        gb_own[b] = total
        gc_send[b] = total.astype(BF16)
        c_copies[b] = []
        for d in range(1, nz):
            to = zpeer(d)
            safe = jnp.minimum(to, owners - 1)
            copy = remote(gc_send.at[b, span(safe), :], gc_recv.at[b, d], c_ss.at[b, d], c_rs.at[b, d], {"nodes": to})
            pl.when(to < owners)(copy.start)
            c_copies[b].append(copy)

    def stage_d(b):
        @pl.when(z < owners)
        def reduce():
            me = jnp.minimum(z, owners - 1)
            total = gb_own[b, span(me), :]
            for d in range(1, nz):
                c_copies[b][d - 1].wait_recv()
                total = total + gc_recv[b, d].astype(F32)
            gd[b, r, span(me), :] = total.astype(BF16)

        d_copies[b] = []
        me = jnp.minimum(z, owners - 1)
        for d in range(1, nz):
            to = zpeer(d)
            copy = remote(
                gd.at[b, r, span(me), :], gd.at[b, r, span(me), :], d_ss.at[b, d], d_rs.at[b, d], {"nodes": to}
            )
            pl.when(z < owners)(copy.start)
            d_copies[b].append(copy)

    def stage_e(b):
        for d in range(1, nz):
            pl.when(zfrom(d) < owners)(d_copies[b][d - 1].wait_recv)
        e_copies[b] = remote(gd.at[b, r], gd.at[b, r], e_ss.at[b], e_rs.at[b], sib)
        e_copies[b].start()
        write(b, r, mine)

    def write(b, c, at):
        l, w = blocks[b]
        wg_ref[:, l, w, at] = gd[b, c].astype(F32)

    def finish(b):
        e_copies[b].wait_recv()
        write(b, 1 - r, other)

    upstream = None
    for l in reversed(range(layers)):
        first = 2 * (layers - 1 - l)
        up = cot_ref[0].astype(F32) if upstream is None else upstream
        before = before_s[l]
        s = 1.0 / (1.0 + jnp.exp(-before))
        slope = (up * (s * (1.0 + before * (1.0 - s)))).astype(BF16)
        slope_s[l] = slope
        rsend[l] = mm(adj_t[rows:, :], slope).astype(BF16).reshape(2, tile, width)
        halo_start(rcopies[l])
        if first > 0:
            stage_a(first - 1)
        stage_a(first)
        own_s[...] = mm(adj_t[0:rows, :], slope)
        dself = mm_bt(slope, wfull[l, 0])
        if first > 0:
            stage_b(first - 1)
            stage_c(first - 2)
        stage_b(first)
        halo_wait(rcopies[l])
        for t in range(tiles):
            at = pl.ds(t * tile, tile)
            part_sum = own_s[at, :]
            for k in range(2):
                part_sum = part_sum + jnp.where(hs_ref[0, k, 0] == t, 1.0, 0.0).astype(F32) * rrecv[l, k].astype(F32)
            back_s[l, at, :] = part_sum.astype(BF16)
        if l == 0:
            stage_a(first + 1)
        dnormed = dself + mm_bt(back_s[l], wfull[l, 1])
        wide = xs[l].reshape(rows, width).astype(F32)
        inv = inv_s[l]
        hg_own[l : l + 1, :] = jnp.sum(dnormed * wide * inv, axis=0, keepdims=True)
        if l > 0:
            scaled = dnormed * gains_ref[l : l + 1, :]
            mean_part = jnp.mean(scaled * wide, axis=-1, keepdims=True)
            upstream = up + inv * scaled - wide * (inv * inv * inv) * mean_part

    ha = remote(hg_own, hg_a, h_ss.at[0], h_rs.at[0], sib)
    ha.start()
    n = len(blocks)
    stage_b(n - 1)
    for b in range(n - 1):
        if b not in c_copies:
            stage_c(b)
    ha.wait_recv()
    hg_b[xi] = hg_own[...] + hg_a[...]
    hb = []
    for d in range(1, nx):
        copy = remote(hg_b.at[xi], hg_b.at[xi], h_ss.at[d], h_rs.at[d], {"fsdp": xpeer(d)})
        copy.start()
        hb.append(copy)
    stage_d(0)
    stage_c(n - 1)
    for d in range(1, nx):
        remote(hg_b.at[xfrom(d)], hg_b.at[xfrom(d)], h_ss.at[d], h_rs.at[d], {"fsdp": xpeer(d)}).wait_recv()
    hsum = hg_b[0]
    for i in range(1, nx):
        hsum = hsum + hg_b[i]
    hg_c[z] = hsum
    hc = []
    for d in range(1, nz):
        copy = remote(hg_c.at[z], hg_c.at[z], h_ss.at[nx + d], h_rs.at[nx + d], {"nodes": zpeer(d)})
        copy.start()
        hc.append(copy)
    for b in range(1, n):
        stage_d(b)
        stage_e(b - 1)
        if b >= 2:
            finish(b - 2)
    stage_e(n - 1)
    finish(n - 2)
    for d in range(1, nz):
        remote(
            hg_c.at[zfrom(d)], hg_c.at[zfrom(d)], h_ss.at[nx + d], h_rs.at[nx + d], {"nodes": zpeer(d)}
        ).wait_recv()
    hsum = hg_c[0]
    for i in range(1, nz):
        hsum = hsum + hg_c[i]
    gg_ref[...] = hsum
    finish(n - 1)

    for g in gathers + forwards + hb + hc + [ha]:
        g.wait_send()
    for b in range(n):
        a_copies[b].wait_send()
        for copy in b_copies[b]:
            copy.wait_send()
        for d in range(1, nz):
            pl.when(zpeer(d) < owners)(c_copies[b][d - 1].wait_send)
            pl.when(z < owners)(d_copies[b][d - 1].wait_send)
        e_copies[b].wait_send()


def solution(mesh):
    nz, nx = mesh.shape["nodes"], mesh.shape["fsdp"]

    def body(features, cotangent, weights, gains, tile_pairs, halo_send, entry_counts, tile_values):
        layers, _, depth, width = weights.shape
        tile = tile_values.shape[-1]
        _, rows, _ = features.shape
        tiles = rows // tile
        cols = tiles + 2
        half = width // 2
        nb = 2 * layers
        chunk = max(16, depth // nz)
        owners = depth // chunk
        vmem = pl.BlockSpec(memory_space=pltpu.VMEM)
        smem = pl.BlockSpec(memory_space=pltpu.SMEM)
        dma = pltpu.SemaphoreType.DMA
        scratch = [
            pltpu.VMEM((layers, 2, width, width), BF16),
            pltpu.VMEM((layers, tiles, tile, width), BF16),
            pltpu.VMEM((layers, rows, 1), F32),
            pltpu.VMEM((layers, rows, width), BF16),
            pltpu.VMEM((layers, rows, width), F32),
            pltpu.VMEM((rows, cols * tile), BF16),
            pltpu.VMEM((cols * tile, rows), BF16),
            pltpu.VMEM((cols * tile, width), BF16),
            pltpu.VMEM((layers, 2, tile, width), BF16),
            pltpu.VMEM((layers, 2, tile, width), BF16),
            pltpu.VMEM((layers, 2, tile, width), BF16),
            pltpu.VMEM((layers, 2, tile, width), BF16),
            pltpu.VMEM((layers, rows, width), BF16),
            pltpu.VMEM((layers, rows, width), BF16),
            pltpu.VMEM((rows, width), F32),
            pltpu.VMEM((nb, width, half), BF16),
            pltpu.VMEM((nb, width, half), BF16),
            pltpu.VMEM((nb, width, half), F32),
            pltpu.VMEM((nb, nx, depth, half), BF16),
            pltpu.VMEM((nb, nx, depth, half), BF16),
            pltpu.VMEM((nb, depth, half), F32),
            pltpu.VMEM((nb, depth, half), BF16),
            pltpu.VMEM((nb, nz, chunk, half), BF16),
            pltpu.VMEM((nb, 2, depth, half), BF16),
            pltpu.VMEM((layers, width), F32),
            pltpu.VMEM((layers, width), F32),
            pltpu.VMEM((nx, layers, width), F32),
            pltpu.VMEM((nz, layers, width), F32),
            dma((layers, nx)), dma((layers, nx)),
            dma((layers, nx)), dma((layers, nx)),
            dma((layers, 2)), dma((layers, 2)),
            dma((layers, 2)), dma((layers, 2)),
            dma((nb,)), dma((nb,)),
            dma((nb, nx)), dma((nb, nx)),
            dma((nb, nz)), dma((nb, nz)),
            dma((nb, nz)), dma((nb, nz)),
            dma((nb,)), dma((nb,)),
            dma((nx + nz,)), dma((nx + nz,)),
        ]
        return pl.pallas_call(
            functools.partial(kernel, nz, nx, chunk, owners),
            out_shape=(
                jax.ShapeDtypeStruct(features.shape, BF16),
                jax.ShapeDtypeStruct((depth, layers, 2, width), F32),
                jax.ShapeDtypeStruct((layers, width), F32),
            ),
            in_specs=[vmem, vmem, vmem, vmem, smem, smem, smem, vmem],
            out_specs=(vmem, vmem, vmem),
            scratch_shapes=scratch,
            compiler_params=pltpu.CompilerParams(
                collective_id=0, has_side_effects=True, vmem_limit_bytes=56 * 1024 * 1024
            ),
        )(features, cotangent, weights, gains, tile_pairs, halo_send, entry_counts, tile_values)

    placed = (
        P(("cases", "fsdp", "rep"), "nodes", None),
        P(("cases", "fsdp", "rep"), "nodes", None),
        P(None, None, "fsdp", None),
        P(),
        P("nodes", None, None),
        P("nodes", None, None),
        P("nodes"),
        P("nodes", None, None, None),
    )
    return jax.shard_map(
        body,
        mesh=mesh,
        in_specs=placed,
        out_specs=(
            P(("cases", "fsdp", "rep"), "nodes", None),
            P("fsdp", "cases", None, None),
            P("cases", None),
        ),
        check_vma=False,
    )
```

time: 540 us -> 71.5 us (0.13); the launches traced: 534 us -> 71.2 us
  starting transfers between devices: 233 us -> 0 us
  waiting for transfers between devices: 162 us -> 0 us
  Pallas kernels: 0 us -> 62.7 us
  loops' own time: 39.1 us -> 0 us
  blocking collectives: 33.5 us -> 0 us
  matrix products: 19 us -> 0 us
  between operations: 18.2 us -> 1.29 us
  local copies, waits for them, and re-layouts: 22.8 us -> 7.19 us
  other arithmetic: 6.09 us -> 0 us
    ppermute x8 -> x0, starting transfers between devices: 233 us -> none  [the longest x4 227 us: with_halo(): before = lax.ppermute(last, axis, up)]
    reduce_scatter x1 -> x0, waiting for transfers between devices: 93 us -> none  [body(): lax.psum_scatter(jnp.concatenate(blocks, axis=1).astype(jnp.bfloat16), 'f...]
    pallas_call x0 -> x1, Pallas kernels: none -> 62.7 us  [body(): pl.pallas_call(functools.partial(kernel, nz, nx, chunk, owners), out_shap...]
    another operation x4 -> x0, loops' own time: 39.1 us -> none  [tile_sweep(): return lax.fori_loop(0, count, step, jnp.zeros(shape, jnp.float32))]
    psum x1 -> x0, blocking collectives: 33.5 us -> none  [body(): gain_grads = lax.psum(jnp.stack(gain_pieces), ('nodes', 'fsdp', 'rep'))]
    psum x1 -> x0, waiting for transfers between devices: 30.9 us -> none  [body(): weight_sum = lax.psum(reduced_rows, ('nodes', 'rep'))]
    all_gather x2 -> x0, waiting for transfers between devices: 19.2 us -> none  [body(): lax.all_gather(pair, 'fsdp', axis=1, tiled=True)]
    dot_general x20 -> x0, matrix products: 19 us -> none  [the longest x4 4.19 us: step(): jnp.einsum('ij,sjd->sid', tile_matrix, source_tile, preferred_element_typ...]
  transfers between devices with their start and end apart: 12 -> 0, of which waited for: 9 -> 0; matrix products, arithmetic and copies ran while one was open for 2% -> 0% of each run, Pallas kernels for 0% -> 0%
where the time goes in v1:
time: 71.5 us; the launch traced here: 71.2 us
  Pallas kernels  62.7 us (88%)
  local copies, waits for them, and re-layouts  7.19 us (10%)
  between operations  1.29 us (2%)
    pallas_call x1, Pallas kernels, body(): pl.pallas_call(functools.partial(kernel, nz, nx, chunk, owners), out_shap...  62.7 us
    unnamed x6, local copies, waits for them, and re-layouts  7.19 us

profile of v1, /device:TPU:0, one launch (start us, length us, event | category | flops | bytes accessed | tf_op | source)
XLA Modules:
  0.0 71.2 jit_solution(2860877835365274225)
XLA Ops:
  1.3 1.3 %copy.11.hs_ref = s32[1,2,1]{2,1,0:T(2,128)} copy(s32[1,2,1]{1,2,0:T(1,128)} %param.13) | data formatting | bytes 16 | tf_op args[5]
  2.6 62.7 %shard_map.103 = (bf16[1,256,512]{2,1,0:T(8,128)(2,1)}, f32[256,2,2,512]{3,2,1,0:T(2,128)}, f32[2,512]{1,0:T(2,128)}) custom-call(bf16[1,256,512]{2,1,0:T(8,128)(2,1)} %x_ref.1, bf16[1,256,512]{2,1,0:T(8,128)(2,1)} %cot_ref.1, bf16[2,2,256,512]{3,2,1,0:T(8,128)(2,1)} %w_ref.1, f32[2,512]{1,0:T(2,128)} %gains_ref.1, s32[1,2,12]{2,1,0:T(2,128)} %pairs_ref.1, ...), custom_call_target="tpu_custom_call" | custom-call | tf_op jit(solution)/shard_map/pallas_call | solution.py:413
  65.3 1.7 %copy.16 = bf16[1,256,512]{2,1,0:T(8,128)(2,1)} copy(bf16[1,256,512]{2,1,0:T(8,128)(2,1)} %get-tuple-element.6) | data formatting | bytes 524288
  66.9 0.0 copy-start
  66.9 3.6 %copy.17 = f32[256,2,2,512]{3,2,1,0:T(2,128)} copy(f32[256,2,2,512]{3,2,1,0:T(2,128)} %get-tuple-element.7) | data formatting | bytes 4194304
  70.6 0.0 copy-done
  70.6 0.6 copy.18
Async XLA Ops:
  66.9 3.6 %copy-start = (f32[2,512]{1,0:T(2,128)S(1)}, f32[2,512]{1,0:T(2,128)}, u32[]{:S(2)}) copy-start(f32[2,512]{1,0:T(2,128)} %get-tuple-element.8) | copy-start | bytes 12292

commit v2 on v1

--- a/solution.py
+++ b/solution.py
@@ -26,12 +26,12 @@
 
 
 def kernel(
-    nz, nx, chunk, owners,
+    nz, nx,
     x_ref, cot_ref, w_ref, gains_ref, pairs_ref, hs_ref, cnt_ref, tv_ref,
-    out_ref, wg_ref, gg_ref,
+    out_ref, gd, gg_ref,
     wfull, xs, inv_s, normed_s, before_s, adj, adj_t, msgs,
     xsend, xrecv, rsend, rrecv, slope_s, back_s, own_s,
-    ga_send, ga_recv, ga_own, gb_send, gb_recv, gb_own, gc_send, gc_recv, gd,
+    ga_send, ga_recv, ga_own, gb_send, gb_recv, gb_own, z_send, z_recv, z_swap,
     hg_own, hg_a, hg_b, hg_c,
     w_ss, w_rs, f_ss, f_rs, x_ss, x_rs, r_ss, r_rs,
     a_ss, a_rs, b_ss, b_rs, c_ss, c_rs, d_ss, d_rs, e_ss, e_rs, h_ss, h_rs,
@@ -106,7 +106,7 @@
                 rrecv[l, k] = jnp.zeros((tile, width), BF16)
 
     for k in range(2):
-        xsend[0, k] = xs[0, hs_ref[0, k, 0]]
+        xsend[0, k] = xs[0, hs_ref[k]]
 
     for l in range(layers):
         for w in range(2):
@@ -176,7 +176,7 @@
         if l + 1 < layers:
             xs[l + 1] = new.reshape(tiles, tile, width)
             for k in range(2):
-                xsend[l + 1, k] = xs[l + 1, hs_ref[0, k, 0]]
+                xsend[l + 1, k] = xs[l + 1, hs_ref[k]]
             halo_start(xcopies[l + 1])
         else:
             out_ref[0] = new
@@ -185,7 +185,7 @@
     other = pl.ds(pl.multiple_of((1 - r) * half, half), half)
     blocks = [(l, w) for l in reversed(range(layers)) for w in range(2)]
 
-    a_copies, b_copies, c_copies, d_copies, e_copies = {}, {}, {}, {}, {}
+    a_copies, b_copies, c_copies, e_copies = {}, {}, {}, {}
 
     def stage_a(b):
         l, w = blocks[b]
@@ -208,8 +208,21 @@
         at = pl.ds(pl.multiple_of(xi * depth, depth), depth)
         gb_own[b] = ga_own[b, at, :] + ga_recv[b, at, :].astype(F32)
 
-    def span(owner):
-        return pl.ds(pl.multiple_of(owner * chunk, chunk), chunk)
+    lower_half = z < nz // 2
+    outermost = (z == 0) | (z == nz - 1)
+    middle = (z == nz // 2 - 1) | (z == nz // 2)
+    inner = {"nodes": jnp.where(lower_half, z + 1, z - 1)}
+    outer = {"nodes": jnp.clip(jnp.where(lower_half, z - 1, z + 1), 0, nz - 1)}
+
+    def inward(b):
+        step = remote(z_send.at[b], z_recv.at[b], c_ss.at[b, 0], c_rs.at[b, 0], inner)
+        swap = remote(z_send.at[b], z_swap.at[b], c_ss.at[b, 1], c_rs.at[b, 1], inner)
+        return step, swap
+
+    def push(b):
+        step, swap = inward(b)
+        pl.when(middle)(swap.start)
+        pl.when(jnp.logical_not(middle))(step.start)
 
     def stage_c(b):
         total = gb_own[b]
@@ -217,49 +230,37 @@
             b_copies[b][d - 1].wait_recv()
             total = total + gb_recv[b, d].astype(F32)
         gb_own[b] = total
-        gc_send[b] = total.astype(BF16)
-        c_copies[b] = []
-        for d in range(1, nz):
-            to = zpeer(d)
-            safe = jnp.minimum(to, owners - 1)
-            copy = remote(gc_send.at[b, span(safe), :], gc_recv.at[b, d], c_ss.at[b, d], c_rs.at[b, d], {"nodes": to})
-            pl.when(to < owners)(copy.start)
-            c_copies[b].append(copy)
+
+        @pl.when(outermost)
+        def begin():
+            z_send[b] = total.astype(BF16)
+            push(b)
+
+        c_copies[b] = True
+
+    def stage_m(b):
+        @pl.when(jnp.logical_not(outermost))
+        def add():
+            inward(b)[0].wait_recv()
+            z_send[b] = (gb_own[b] + z_recv[b].astype(F32)).astype(BF16)
+            push(b)
+
+    def outward(b):
+        return remote(gd.at[b, r], gd.at[b, r], d_ss.at[b], d_rs.at[b], outer)
 
     def stage_d(b):
-        @pl.when(z < owners)
-        def reduce():
-            me = jnp.minimum(z, owners - 1)
-            total = gb_own[b, span(me), :]
-            for d in range(1, nz):
-                c_copies[b][d - 1].wait_recv()
-                total = total + gc_recv[b, d].astype(F32)
-            gd[b, r, span(me), :] = total.astype(BF16)
-
-        d_copies[b] = []
-        me = jnp.minimum(z, owners - 1)
-        for d in range(1, nz):
-            to = zpeer(d)
-            copy = remote(
-                gd.at[b, r, span(me), :], gd.at[b, r, span(me), :], d_ss.at[b, d], d_rs.at[b, d], {"nodes": to}
-            )
-            pl.when(z < owners)(copy.start)
-            d_copies[b].append(copy)
-
-    def stage_e(b):
-        for d in range(1, nz):
-            pl.when(zfrom(d) < owners)(d_copies[b][d - 1].wait_recv)
+        @pl.when(middle)
+        def total():
+            inward(b)[1].wait_recv()
+            gd[b, r] = (z_send[b].astype(F32) + z_swap[b].astype(F32)).astype(BF16)
+
+        pl.when(jnp.logical_not(middle))(outward(b).wait_recv)
+        pl.when(jnp.logical_not(outermost))(outward(b).start)
         e_copies[b] = remote(gd.at[b, r], gd.at[b, r], e_ss.at[b], e_rs.at[b], sib)
         e_copies[b].start()
-        write(b, r, mine)
-
-    def write(b, c, at):
-        l, w = blocks[b]
-        wg_ref[:, l, w, at] = gd[b, c].astype(F32)
 
     def finish(b):
         e_copies[b].wait_recv()
-        write(b, 1 - r, other)
 
     upstream = None
     for l in reversed(range(layers)):
@@ -285,7 +286,7 @@
             at = pl.ds(t * tile, tile)
             part_sum = own_s[at, :]
             for k in range(2):
-                part_sum = part_sum + jnp.where(hs_ref[0, k, 0] == t, 1.0, 0.0).astype(F32) * rrecv[l, k].astype(F32)
+                part_sum = part_sum + jnp.where(hs_ref[k] == t, 1.0, 0.0).astype(F32) * rrecv[l, k].astype(F32)
             back_s[l, at, :] = part_sum.astype(BF16)
         if l == 0:
             stage_a(first + 1)
@@ -305,6 +306,8 @@
     for b in range(n - 1):
         if b not in c_copies:
             stage_c(b)
+        if b < n - 2:
+            stage_m(b)
     ha.wait_recv()
     hg_b[xi] = hg_own[...] + hg_a[...]
     hb = []
@@ -312,8 +315,9 @@
         copy = remote(hg_b.at[xi], hg_b.at[xi], h_ss.at[d], h_rs.at[d], {"fsdp": xpeer(d)})
         copy.start()
         hb.append(copy)
+    stage_c(n - 1)
     stage_d(0)
-    stage_c(n - 1)
+    stage_m(n - 2)
     for d in range(1, nx):
         remote(hg_b.at[xfrom(d)], hg_b.at[xfrom(d)], h_ss.at[d], h_rs.at[d], {"fsdp": xpeer(d)}).wait_recv()
     hsum = hg_b[0]
@@ -325,13 +329,12 @@
         copy = remote(hg_c.at[z], hg_c.at[z], h_ss.at[nx + d], h_rs.at[nx + d], {"nodes": zpeer(d)})
         copy.start()
         hc.append(copy)
-    for b in range(1, n):
+    stage_d(1)
+    stage_m(n - 1)
+    for b in range(2, n):
         stage_d(b)
-        stage_e(b - 1)
-        if b >= 2:
-            finish(b - 2)
-    stage_e(n - 1)
-    finish(n - 2)
+    for b in range(n - 1):
+        finish(b)
     for d in range(1, nz):
         remote(
             hg_c.at[zfrom(d)], hg_c.at[zfrom(d)], h_ss.at[nx + d], h_rs.at[nx + d], {"nodes": zpeer(d)}
@@ -348,10 +351,40 @@
         a_copies[b].wait_send()
         for copy in b_copies[b]:
             copy.wait_send()
-        for d in range(1, nz):
-            pl.when(zpeer(d) < owners)(c_copies[b][d - 1].wait_send)
-            pl.when(z < owners)(d_copies[b][d - 1].wait_send)
+        step, swap = inward(b)
+        pl.when(middle)(swap.wait_send)
+        pl.when(jnp.logical_not(middle))(step.wait_send)
+        pl.when(jnp.logical_not(outermost))(outward(b).wait_send)
         e_copies[b].wait_send()
+
+
+def expand_kernel(out_in, gd, gg_in, out_ref, wg_ref, gg_ref):
+    out_ref[...] = out_in[...]
+    gg_ref[...] = gg_in[...]
+    layers, half = wg_ref.shape[1], gd.shape[-1]
+    for b in range(gd.shape[0]):
+        l, w = layers - 1 - b // 2, b % 2
+        for c in range(2):
+            wg_ref[:, l, w, c * half : (c + 1) * half] = gd[b, c].astype(F32)
+
+
+def expand(out, gd, gg):
+    nb, _, depth, half = gd.shape
+    layers, width = gg.shape
+    steps = 4
+    rows = pl.BlockSpec((1, out.shape[1] // steps, width), lambda i: (0, i, 0))
+    whole = pl.BlockSpec((layers, width), lambda i: (0, 0))
+    return pl.pallas_call(
+        expand_kernel,
+        grid=(steps,),
+        out_shape=(
+            jax.ShapeDtypeStruct(out.shape, out.dtype),
+            jax.ShapeDtypeStruct((depth, layers, 2, width), F32),
+            jax.ShapeDtypeStruct(gg.shape, F32),
+        ),
+        in_specs=[rows, pl.BlockSpec((nb, 2, depth // steps, half), lambda i: (0, 0, i, 0)), whole],
+        out_specs=(rows, pl.BlockSpec((depth // steps, layers, 2, width), lambda i: (i, 0, 0, 0)), whole),
+    )(out, gd, gg)
 
 
 def solution(mesh):
@@ -365,8 +398,6 @@
         cols = tiles + 2
         half = width // 2
         nb = 2 * layers
-        chunk = max(16, depth // nz)
-        owners = depth // chunk
         vmem = pl.BlockSpec(memory_space=pltpu.VMEM)
         smem = pl.BlockSpec(memory_space=pltpu.SMEM)
         dma = pltpu.SemaphoreType.DMA
@@ -393,8 +424,8 @@
             pltpu.VMEM((nb, nx, depth, half), BF16),
             pltpu.VMEM((nb, depth, half), F32),
             pltpu.VMEM((nb, depth, half), BF16),
-            pltpu.VMEM((nb, nz, chunk, half), BF16),
-            pltpu.VMEM((nb, 2, depth, half), BF16),
+            pltpu.VMEM((nb, depth, half), BF16),
+            pltpu.VMEM((nb, depth, half), BF16),
             pltpu.VMEM((layers, width), F32),
             pltpu.VMEM((layers, width), F32),
             pltpu.VMEM((nx, layers, width), F32),
@@ -405,16 +436,16 @@
             dma((layers, 2)), dma((layers, 2)),
             dma((nb,)), dma((nb,)),
             dma((nb, nx)), dma((nb, nx)),
-            dma((nb, nz)), dma((nb, nz)),
-            dma((nb, nz)), dma((nb, nz)),
+            dma((nb, 2)), dma((nb, 2)),
+            dma((nb,)), dma((nb,)),
             dma((nb,)), dma((nb,)),
             dma((nx + nz,)), dma((nx + nz,)),
         ]
-        return pl.pallas_call(
-            functools.partial(kernel, nz, nx, chunk, owners),
+        kept = pl.pallas_call(
+            functools.partial(kernel, nz, nx),
             out_shape=(
                 jax.ShapeDtypeStruct(features.shape, BF16),
-                jax.ShapeDtypeStruct((depth, layers, 2, width), F32),
+                jax.ShapeDtypeStruct((nb, 2, depth, half), BF16),
                 jax.ShapeDtypeStruct((layers, width), F32),
             ),
             in_specs=[vmem, vmem, vmem, vmem, smem, smem, smem, vmem],
@@ -423,7 +454,8 @@
             compiler_params=pltpu.CompilerParams(
                 collective_id=0, has_side_effects=True, vmem_limit_bytes=56 * 1024 * 1024
             ),
-        )(features, cotangent, weights, gains, tile_pairs, halo_send, entry_counts, tile_values)
+        )(features, cotangent, weights, gains, tile_pairs, halo_send.reshape(-1), entry_counts, tile_values)
+        return expand(*kept)
 
     placed = (
         P(("cases", "fsdp", "rep"), "nodes", None),

time: 71.5 us -> 63.4 us (0.89)
  local copies, waits for them, and re-layouts: 7.19 us -> 0 us
  Pallas kernels: 62.7 us -> 61.9 us
    unnamed x6 -> x0, local copies, waits for them, and re-layouts: 7.19 us -> none
    pallas_call x1 -> x2, Pallas kernels: 62.7 us -> 61.9 us  [the longest x1 58 us: body(): pl.pallas_call(functools.partial(kernel, nz, nx), out_shape=(jax.ShapeDty...]
where the time goes in v2:
time: 63.4 us; the launch traced here: 63.2 us
  Pallas kernels  61.9 us (98%)
  between operations  1.29 us (2%)
    pallas_call x1, Pallas kernels, body(): pl.pallas_call(functools.partial(kernel, nz, nx), out_shape=(jax.ShapeDty...  58 us
    pallas_call x1, Pallas kernels, expand(): pl.pallas_call(expand_kernel, grid=(steps,), out_shape=(jax.ShapeDtypeStr...  3.95 us

profile of v2, /device:TPU:0, one launch (start us, length us, event | category | flops | bytes accessed | tf_op | source)
XLA Modules:
  0.0 63.2 jit_solution(16170819283220758770)
XLA Ops:
  1.3 58.0 %shard_map.103 = (bf16[1,256,512]{2,1,0:T(8,128)(2,1)}, bf16[4,2,256,256]{3,2,1,0:T(8,128)(2,1)}, f32[2,512]{1,0:T(2,128)}) custom-call(bf16[1,256,512]{2,1,0:T(8,128)(2,1)} %x_ref.1, bf16[1,256,512]{2,1,0:T(8,128)(2,1)} %cot_ref.1, bf16[2,2,256,512]{3,2,1,0:T(8,128)(2,1)} %w_ref.1, f32[2,512]{1,0:T(2,128)} %gains_ref.1, s32[1,2,12]{2,1,0:T(2,128)} %pairs_ref.1, ...), custom_call_target="tpu_custom_call" | custom-call | tf_op jit(solution)/shard_map/pallas_call | solution.py:444
  59.3 4.0 %shard_map.104 = (bf16[1,256,512]{2,1,0:T(8,128)(2,1)}, f32[256,2,2,512]{3,2,1,0:T(2,128)}, f32[2,512]{1,0:T(2,128)}) custom-call(bf16[1,256,512]{2,1,0:T(8,128)(2,1)} %get-tuple-element.6.out_in, bf16[4,2,256,256]{3,2,1,0:T(8,128)(2,1)} %get-tuple-element.7.gd, f32[2,512]{1,0:T(2,128)} %get-tuple-element.8.gg_in), custom_call_target="tpu_custom_call" | custom-call | tf_op jit(solution)/shard_map/pallas_call | solution.py:377

commit v3 on v2

--- a/solution.py
+++ b/solution.py
@@ -186,6 +186,7 @@
     blocks = [(l, w) for l in reversed(range(layers)) for w in range(2)]
 
     a_copies, b_copies, c_copies, e_copies = {}, {}, {}, {}
+    m_done = set()
 
     def stage_a(b):
         l, w = blocks[b]
@@ -214,13 +215,16 @@
     inner = {"nodes": jnp.where(lower_half, z + 1, z - 1)}
     outer = {"nodes": jnp.clip(jnp.where(lower_half, z - 1, z + 1), 0, nz - 1)}
 
-    def inward(b):
-        step = remote(z_send.at[b], z_recv.at[b], c_ss.at[b, 0], c_rs.at[b, 0], inner)
-        swap = remote(z_send.at[b], z_swap.at[b], c_ss.at[b, 1], c_rs.at[b, 1], inner)
+    pieces = [slice(h * depth // 2, (h + 1) * depth // 2) for h in range(2)]
+
+    def inward(b, h):
+        at = pieces[h]
+        step = remote(z_send.at[b, at], z_recv.at[b, at], c_ss.at[b, h], c_rs.at[b, h], inner)
+        swap = remote(z_send.at[b, at], z_swap.at[b, at], c_ss.at[b, 2 + h], c_rs.at[b, 2 + h], inner)
         return step, swap
 
-    def push(b):
-        step, swap = inward(b)
+    def push(b, h):
+        step, swap = inward(b, h)
         pl.when(middle)(swap.start)
         pl.when(jnp.logical_not(middle))(step.start)
 
@@ -234,33 +238,44 @@
         @pl.when(outermost)
         def begin():
             z_send[b] = total.astype(BF16)
-            push(b)
+            for h in range(2):
+                push(b, h)
 
         c_copies[b] = True
 
     def stage_m(b):
+        m_done.add(b)
+
         @pl.when(jnp.logical_not(outermost))
         def add():
-            inward(b)[0].wait_recv()
-            z_send[b] = (gb_own[b] + z_recv[b].astype(F32)).astype(BF16)
-            push(b)
-
-    def outward(b):
-        return remote(gd.at[b, r], gd.at[b, r], d_ss.at[b], d_rs.at[b], outer)
+            for h, at in enumerate(pieces):
+                inward(b, h)[0].wait_recv()
+                z_send[b, at] = (gb_own[b, at] + z_recv[b, at].astype(F32)).astype(BF16)
+                push(b, h)
+
+    def outward(b, h):
+        place = gd.at[b, r, pieces[h]]
+        return remote(place, place, d_ss.at[b, h], d_rs.at[b, h], outer)
 
     def stage_d(b):
-        @pl.when(middle)
-        def total():
-            inward(b)[1].wait_recv()
-            gd[b, r] = (z_send[b].astype(F32) + z_swap[b].astype(F32)).astype(BF16)
-
-        pl.when(jnp.logical_not(middle))(outward(b).wait_recv)
-        pl.when(jnp.logical_not(outermost))(outward(b).start)
-        e_copies[b] = remote(gd.at[b, r], gd.at[b, r], e_ss.at[b], e_rs.at[b], sib)
-        e_copies[b].start()
+        e_copies[b] = []
+        for h, at in enumerate(pieces):
+
+            @pl.when(middle)
+            def total(h=h, at=at):
+                inward(b, h)[1].wait_recv()
+                gd[b, r, at] = (z_send[b, at].astype(F32) + z_swap[b, at].astype(F32)).astype(BF16)
+
+            pl.when(jnp.logical_not(middle))(outward(b, h).wait_recv)
+            pl.when(jnp.logical_not(outermost))(outward(b, h).start)
+            place = gd.at[b, r, at]
+            copy = remote(place, place, e_ss.at[b, h], e_rs.at[b, h], sib)
+            copy.start()
+            e_copies[b].append(copy)
 
     def finish(b):
-        e_copies[b].wait_recv()
+        for copy in e_copies[b]:
+            copy.wait_recv()
 
     upstream = None
     for l in reversed(range(layers)):
@@ -290,6 +305,9 @@
             back_s[l, at, :] = part_sum.astype(BF16)
         if l == 0:
             stage_a(first + 1)
+        if first > 0:
+            stage_c(first - 1)
+            stage_m(first - 2)
         dnormed = dself + mm_bt(back_s[l], wfull[l, 1])
         wide = xs[l].reshape(rows, width).astype(F32)
         inv = inv_s[l]
@@ -306,7 +324,7 @@
     for b in range(n - 1):
         if b not in c_copies:
             stage_c(b)
-        if b < n - 2:
+        if b < n - 2 and b not in m_done:
             stage_m(b)
     ha.wait_recv()
     hg_b[xi] = hg_own[...] + hg_a[...]
@@ -351,11 +369,12 @@
         a_copies[b].wait_send()
         for copy in b_copies[b]:
             copy.wait_send()
-        step, swap = inward(b)
-        pl.when(middle)(swap.wait_send)
-        pl.when(jnp.logical_not(middle))(step.wait_send)
-        pl.when(jnp.logical_not(outermost))(outward(b).wait_send)
-        e_copies[b].wait_send()
+        for h in range(2):
+            step, swap = inward(b, h)
+            pl.when(middle)(swap.wait_send)
+            pl.when(jnp.logical_not(middle))(step.wait_send)
+            pl.when(jnp.logical_not(outermost))(outward(b, h).wait_send)
+            e_copies[b][h].wait_send()
 
 
 def expand_kernel(out_in, gd, gg_in, out_ref, wg_ref, gg_ref):
@@ -436,9 +455,9 @@
             dma((layers, 2)), dma((layers, 2)),
             dma((nb,)), dma((nb,)),
             dma((nb, nx)), dma((nb, nx)),
+            dma((nb, 4)), dma((nb, 4)),
             dma((nb, 2)), dma((nb, 2)),
-            dma((nb,)), dma((nb,)),
-            dma((nb,)), dma((nb,)),
+            dma((nb, 2)), dma((nb, 2)),
             dma((nx + nz,)), dma((nx + nz,)),
         ]
         kept = pl.pallas_call(

time: 63.4 us -> 61.6 us (0.972)
  Pallas kernels: 61.9 us -> 60.1 us
    pallas_call x1, Pallas kernels: 58 us -> 56.1 us  [body(): pl.pallas_call(functools.partial(kernel, nz, nx), out_shape=(jax.ShapeDty...]
where the time goes in v3:
time: 61.6 us; the launch traced here: 61.4 us
  Pallas kernels  60.1 us (98%)
  between operations  1.29 us (2%)
    pallas_call x1, Pallas kernels, body(): pl.pallas_call(functools.partial(kernel, nz, nx), out_shape=(jax.ShapeDty...  56.1 us
    pallas_call x1, Pallas kernels, expand(): pl.pallas_call(expand_kernel, grid=(steps,), out_shape=(jax.ShapeDtypeStr...  3.95 us

profile of v3, /device:TPU:0, one launch (start us, length us, event | category | flops | bytes accessed | tf_op | source)
XLA Modules:
  0.0 61.4 jit_solution(1717757428005142680)
XLA Ops:
  1.3 56.1 %shard_map.103 = (bf16[1,256,512]{2,1,0:T(8,128)(2,1)}, bf16[4,2,256,256]{3,2,1,0:T(8,128)(2,1)}, f32[2,512]{1,0:T(2,128)}) custom-call(bf16[1,256,512]{2,1,0:T(8,128)(2,1)} %x_ref.1, bf16[1,256,512]{2,1,0:T(8,128)(2,1)} %cot_ref.1, bf16[2,2,256,512]{3,2,1,0:T(8,128)(2,1)} %w_ref.1, f32[2,512]{1,0:T(2,128)} %gains_ref.1, s32[1,2,12]{2,1,0:T(2,128)} %pairs_ref.1, ...), custom_call_target="tpu_custom_call" | custom-call | tf_op jit(solution)/shard_map/pallas_call | solution.py:463
  57.4 4.0 %shard_map.104 = (bf16[1,256,512]{2,1,0:T(8,128)(2,1)}, f32[256,2,2,512]{3,2,1,0:T(2,128)}, f32[2,512]{1,0:T(2,128)}) custom-call(bf16[1,256,512]{2,1,0:T(8,128)(2,1)} %get-tuple-element.6.out_in, bf16[4,2,256,256]{3,2,1,0:T(8,128)(2,1)} %get-tuple-element.7.gd, f32[2,512]{1,0:T(2,128)} %get-tuple-element.8.gg_in), custom_call_target="tpu_custom_call" | custom-call | tf_op jit(solution)/shard_map/pallas_call | solution.py:396
